TPU v7x, 32 devices: a whole 2x2x4 slice. The times are simulated.
32 devices in a mesh: section: 8 (over z, x), dp: 4 (over y, core).
Axes of the slice: x: 2, y: 2, z: 4, core: 2. Of those that a mesh axis runs over, the one named last changes fastest.
Arguments:
- stream_in: bfloat16 [1024, 2048], P('dp'), may hold values from -6 to 6
- sample_ids: int32 [4, 8], P('dp'), may hold values from 0 to 31
- epoch_buffer: bfloat16 [8, 128, 32, 2048], P('section', 'dp'), may hold values from -8 to 8
- layer_weight: bfloat16 [8, 2048, 2048], P('section', 'dp'), may hold values from -0.125 to 0.125
- top_cotangent: bfloat16 [1024, 2048], P('dp'), may hold values from -6 to 6
Outputs:
- decoded: bfloat16 [8, 1024, 2048], P('section', 'dp')
- weight_grad: float32 [8, 2048, 2048], P('section', 'dp')
Inputs may be any that keep to these rules, and one draw needn't show every extreme that they name: `sample_ids`: an entry of the replica's own pool of 32 samples.
All inputs are finite; a program needn't handle non-finite values.
Results may differ from a plain program's by a relative error of at most 0.035.
Values may be sent and summed in bfloat16 or wider, within the bound.
A program may use at most 128 MiB of HBM per device.

v0:
```python
import jax
import jax.numpy as jnp
from jax import lax
from jax.sharding import PartitionSpec as P

epsilon = 1e-05


def from_behind(value, axis, steps):
    count = lax.axis_size(axis)
    leading, last = (max(0, -steps), min(count, count - steps))
    return lax.ppermute(value, axis, [(source, source + steps) for source in range(leading, last)])


def normalize(values):
    return values * lax.rsqrt(jnp.mean(values * values, axis=-1, keepdims=True) + epsilon)


def encode(output_rows, base_rows):
    bound_rows = 2.0 * jnp.sqrt(
        jnp.mean(output_rows * output_rows, axis=-1, keepdims=True) + epsilon
    )
    delta_rows = jnp.clip(output_rows - base_rows, -bound_rows, bound_rows).astype(jnp.bfloat16)
    return (base_rows + delta_rows.astype(jnp.float32)).astype(jnp.bfloat16)


def local(stream_in, sample_ids, epoch_buffer, layer_weight, top_cotangent):
    sections = lax.axis_size("section")
    position = lax.axis_index("section")
    weight = lax.all_gather(layer_weight[0], "dp", axis=0, tiled=True)
    micro = sample_ids.shape[1]
    tokens_block = epoch_buffer.shape[2]
    width = stream_in.shape[1]
    group = 1
    blocks = micro // group
    block_rows = group * tokens_block
    base_all = jnp.take(epoch_buffer[0], sample_ids[0], axis=0)
    first_blocks = stream_in.reshape(blocks, block_rows, width)
    top_blocks = top_cotangent.reshape(blocks, block_rows, width)
    blank = jnp.zeros((block_rows, width), jnp.bfloat16)
    storage = jnp.zeros((blocks, block_rows, width), jnp.bfloat16)
    steps_total = jnp.arange(blocks + sections - 1, dtype=jnp.int32)

    def forward_step(carry, step_index):
        message, saved, decoded = carry
        block_index = step_index - position
        active_flag = (block_index >= 0) & (block_index < blocks)
        picked = jnp.clip(block_index, 0, blocks - 1)
        first_rows = lax.dynamic_index_in_dim(first_blocks, picked, 0, keepdims=False)
        incoming = jnp.where(position == 0, first_rows, message)

        def run_layer(operands):
            saved_rows, decoded_rows = operands
            values = incoming.astype(jnp.float32)
            normed = normalize(values).astype(jnp.bfloat16)
            output_rows = values + jnp.dot(normed, weight, preferred_element_type=jnp.float32)
            base_rows = lax.dynamic_index_in_dim(base_all, picked, 0, keepdims=False).astype(
                jnp.float32
            )
            encoded = encode(output_rows, base_rows)
            saved_rows = lax.dynamic_update_index_in_dim(saved_rows, incoming, picked, 0)
            decoded_rows = lax.dynamic_update_index_in_dim(decoded_rows, encoded, picked, 0)
            return (encoded, saved_rows, decoded_rows)

        def skip_layer(operands):
            return (blank, operands[0], operands[1])

        outgoing, saved, decoded = lax.cond(active_flag, run_layer, skip_layer, (saved, decoded))
        message = from_behind(outgoing, "section", 1)
        return ((message, saved, decoded), None)

    forward_state, leftover = lax.scan(forward_step, (blank, storage, storage), steps_total)
    saved = forward_state[1]
    decoded = forward_state[2]

    def backward_step(carry, step_index):
        message, cot_blocks = carry
        block_index = step_index - (sections - 1 - position)
        active_flag = (block_index >= 0) & (block_index < blocks)
        picked = jnp.clip(block_index, 0, blocks - 1)
        top_rows = lax.dynamic_index_in_dim(top_blocks, picked, 0, keepdims=False)
        incoming = jnp.where(position == sections - 1, top_rows, message)

        def run_back(cot_rows):
            values = lax.dynamic_index_in_dim(saved, picked, 0, keepdims=False).astype(jnp.float32)
            backward_rows = lax.dot_general(
                incoming, weight, (((1,), (1,)), ((), ())), preferred_element_type=jnp.float32
            )
            through = jax.vjp(normalize, values)[1](backward_rows)[0]
            sending = (incoming.astype(jnp.float32) + through).astype(jnp.bfloat16)
            return (sending, lax.dynamic_update_index_in_dim(cot_rows, incoming, picked, 0))

        def skip_back(cot_rows):
            return (blank, cot_rows)

        outgoing, cot_blocks = lax.cond(active_flag, run_back, skip_back, cot_blocks)
        message = from_behind(outgoing, "section", -1)
        return ((message, cot_blocks), None)

    backward_state, remains = lax.scan(backward_step, (blank, storage), steps_total)
    cot_all = backward_state[1].reshape(-1, width)
    normed_all = normalize(saved.reshape(-1, width).astype(jnp.float32)).astype(jnp.bfloat16)
    gradient = lax.psum_scatter(
        lax.dot_general(
            normed_all, cot_all, (((0,), (0,)), ((), ())), preferred_element_type=jnp.float32
        ).astype(jnp.bfloat16),
        "dp",
        scatter_dimension=0,
        tiled=True,
    ).astype(jnp.float32)
    return (decoded.reshape(1, -1, width), gradient[None])


def solution(mesh):
    in_specs = (
        P("dp", None),
        P("dp", None),
        P("section", "dp", None, None),
        P("section", "dp", None),
        P("dp", None),
    )
    out_specs = (P("section", "dp", None), P("section", "dp", None))
    return jax.shard_map(local, mesh=mesh, in_specs=in_specs, out_specs=out_specs, check_vma=False)
```

profile of v0, /device:TPU:0, one launch (start us, length us, event | category | flops | bytes accessed | tf_op | source)
XLA Modules:
  0.0 605.6 jit_solution(11045995384491468941)
XLA Ops:
  11.6 59.0 %all-gather.3.cloned.1.call-done = bf16[1,2048,2048]{2,1,0:T(8,128)(2,1)} async-done(((bf16[1,512,2048]{2,1,0:T(8,128)(2,1)}), bf16[1,2048,2048]{2,1,0:T(8,128)(2,1)}) %all-gather.3.cloned.1.call-update) | async-done | bytes 8388624 | tf_op jit(solution)/shard_map/all_gather | solution.py:30
  70.9 196.4 %while.32 = (s32[]{:T(128)}, bf16[32,2048]{1,0:T(8,128)(2,1)S(1)}, bf16[8,32,2048]{2,1,0:T(8,128)(2,1)S(1)}, bf16[8,32,2048]{2,1,0:T(8,128)(2,1)S(1)}, s32[15]{0...) while((s32[]{:T(128)}, bf16[32,2048]{1,0:T(8,128)(2,1)S(1)}, ...), condition=%wide.region_5.6_spmd, body=%wide.region_0.5_spmd.sunk | while | flops 269746368 | bytes 10619104 | solution.py:72
  187.8 11.6 %collective-permute-start = (bf16[32,2048]{1,0:T(8,128)(2,1)S(1)}, bf16[32,2048]{1,0:T(8,128)(2,1)S(1)}, u32[]{:S(2)}, u32[]{:S(2)}) collective-permute-start(bf16[32,2048]{1,0:T(8,128)(2,1)S(1)} %get-tuple-element.538), channel_id=1, source_target_pairs={{0,4},{4,8},{8,12},{12,16},{16,20},{20,24},{24,28},{1,5},{5,9},{9,... | collective-permute-start | bytes 393224 | tf_op jit(solution)/shard_map/while/body/eval_jaxpr/ppermute | solution.py:12
  212.1 11.6 %collective-permute-start = (bf16[32,2048]{1,0:T(8,128)(2,1)S(1)}, bf16[32,2048]{1,0:T(8,128)(2,1)S(1)}, u32[]{:S(2)}, u32[]{:S(2)}) collective-permute-start(bf16[32,2048]{1,0:T(8,128)(2,1)S(1)} %get-tuple-element.538), channel_id=1, source_target_pairs={{0,4},{4,8},{8,12},{12,16},{16,20},{20,24},{24,28},{1,5},{5,9},{9,... | collective-permute-start | bytes 393224 | tf_op jit(solution)/shard_map/while/body/eval_jaxpr/ppermute | solution.py:12
  257.5 7.1 %collective-permute-start = (bf16[32,2048]{1,0:T(8,128)(2,1)S(1)}, bf16[32,2048]{1,0:T(8,128)(2,1)S(1)}, u32[]{:S(2)}, u32[]{:S(2)}) collective-permute-start(bf16[32,2048]{1,0:T(8,128)(2,1)S(1)} %get-tuple-element.538), channel_id=1, source_target_pairs={{0,4},{4,8},{8,12},{12,16},{16,20},{20,24},{24,28},{1,5},{5,9},{9,... | collective-permute-start | bytes 393224 | tf_op jit(solution)/shard_map/while/body/eval_jaxpr/ppermute | solution.py:12
  268.2 252.7 %while.33 = (s32[]{:T(128)}, bf16[32,2048]{1,0:T(8,128)(2,1)S(1)}, bf16[8,32,2048]{2,1,0:T(8,128)(2,1)S(1)}, s32[15]{0:T(128)S(1)}, s32[]{:T(128)}, /*index=5*/p...) while((s32[]{:T(128)}, bf16[32,2048]{1,0:T(8,128)(2,1)S(1)}, ...), condition=%wide.region_12.13_spmd, body=%wide.region_7.12_spmd.sunk | while | flops 269353088 | bytes 10618172 | solution.py:100
  270.8 6.8 %collective-permute-done.1 = bf16[32,2048]{1,0:T(8,128)(2,1)S(1)} collective-permute-done((bf16[32,2048]{1,0:T(8,128)(2,1)S(1)}, bf16[32,2048]{1,0:T(8,128)(2,1)S(1)}, u32[]{:S(2)}, u32[]{:S(2)}) %collective-permute-start.1) | collective-permute-done | bytes 131104 | tf_op jit(solution)/shard_map/while/body/eval_jaxpr/ppermute | solution.py:12
  280.2 10.0 %collective-permute-done.1 = bf16[32,2048]{1,0:T(8,128)(2,1)S(1)} collective-permute-done((bf16[32,2048]{1,0:T(8,128)(2,1)S(1)}, bf16[32,2048]{1,0:T(8,128)(2,1)S(1)}, u32[]{:S(2)}, u32[]{:S(2)}) %collective-permute-start.1) | collective-permute-done | bytes 131104 | tf_op jit(solution)/shard_map/while/body/eval_jaxpr/ppermute | solution.py:12
  292.7 6.5 %collective-permute-done.1 = bf16[32,2048]{1,0:T(8,128)(2,1)S(1)} collective-permute-done((bf16[32,2048]{1,0:T(8,128)(2,1)S(1)}, bf16[32,2048]{1,0:T(8,128)(2,1)S(1)}, u32[]{:S(2)}, u32[]{:S(2)}) %collective-permute-start.1) | collective-permute-done | bytes 131104 | tf_op jit(solution)/shard_map/while/body/eval_jaxpr/ppermute | solution.py:12
  301.8 10.5 %collective-permute-done.1 = bf16[32,2048]{1,0:T(8,128)(2,1)S(1)} collective-permute-done((bf16[32,2048]{1,0:T(8,128)(2,1)S(1)}, bf16[32,2048]{1,0:T(8,128)(2,1)S(1)}, u32[]{:S(2)}, u32[]{:S(2)}) %collective-permute-start.1) | collective-permute-done | bytes 131104 | tf_op jit(solution)/shard_map/while/body/eval_jaxpr/ppermute | solution.py:12
  314.9 6.5 %collective-permute-done.1 = bf16[32,2048]{1,0:T(8,128)(2,1)S(1)} collective-permute-done((bf16[32,2048]{1,0:T(8,128)(2,1)S(1)}, bf16[32,2048]{1,0:T(8,128)(2,1)S(1)}, u32[]{:S(2)}, u32[]{:S(2)}) %collective-permute-start.1) | collective-permute-done | bytes 131104 | tf_op jit(solution)/shard_map/while/body/eval_jaxpr/ppermute | solution.py:12
  323.9 9.4 %collective-permute-done.1 = bf16[32,2048]{1,0:T(8,128)(2,1)S(1)} collective-permute-done((bf16[32,2048]{1,0:T(8,128)(2,1)S(1)}, bf16[32,2048]{1,0:T(8,128)(2,1)S(1)}, u32[]{:S(2)}, u32[]{:S(2)}) %collective-permute-start.1) | collective-permute-done | bytes 131104 | tf_op jit(solution)/shard_map/while/body/eval_jaxpr/ppermute | solution.py:12
  335.9 56.2 %collective-permute-done.1 = bf16[32,2048]{1,0:T(8,128)(2,1)S(1)} collective-permute-done((bf16[32,2048]{1,0:T(8,128)(2,1)S(1)}, bf16[32,2048]{1,0:T(8,128)(2,1)S(1)}, u32[]{:S(2)}, u32[]{:S(2)}) %collective-permute-start.1) | collective-permute-done | bytes 131104 | tf_op jit(solution)/shard_map/while/body/eval_jaxpr/ppermute | solution.py:12
  393.3 7.2 %conditional.5 = (bf16[32,2048]{1,0:T(8,128)(2,1)S(1)}, bf16[8,32,2048]{2,1,0:T(8,128)(2,1)S(1)}) conditional(s32[]{:T(128)} %convert_element_type.123, bf16[8,32,2048]{2,1,0:T(8,128)(2,1)S(1)} %get-tuple-element.615, (pred[]{:T(512)}, s32[]{:T(128)}, bf16[8,32,2048]{2,1,0:T(8,128)(2,1)}, bf16[32,2048]{1,0:T(8,128)(2,1)S(1)}, ...), branch_computations={%region_8.8_spmd, %region_9.11_spmd} | conditional | flops 269353088 | bytes 10093621 | solution.py:96
  401.9 6.5 %collective-permute-done.1 = bf16[32,2048]{1,0:T(8,128)(2,1)S(1)} collective-permute-done((bf16[32,2048]{1,0:T(8,128)(2,1)S(1)}, bf16[32,2048]{1,0:T(8,128)(2,1)S(1)}, u32[]{:S(2)}, u32[]{:S(2)}) %collective-permute-start.1) | collective-permute-done | bytes 131104 | tf_op jit(solution)/shard_map/while/body/eval_jaxpr/ppermute | solution.py:12
  409.6 7.2 %conditional.5 = (bf16[32,2048]{1,0:T(8,128)(2,1)S(1)}, bf16[8,32,2048]{2,1,0:T(8,128)(2,1)S(1)}) conditional(s32[]{:T(128)} %convert_element_type.123, bf16[8,32,2048]{2,1,0:T(8,128)(2,1)S(1)} %get-tuple-element.615, (pred[]{:T(512)}, s32[]{:T(128)}, bf16[8,32,2048]{2,1,0:T(8,128)(2,1)}, bf16[32,2048]{1,0:T(8,128)(2,1)S(1)}, ...), branch_computations={%region_8.8_spmd, %region_9.11_spmd} | conditional | flops 269353088 | bytes 10093621 | solution.py:96
  418.1 6.5 %collective-permute-done.1 = bf16[32,2048]{1,0:T(8,128)(2,1)S(1)} collective-permute-done((bf16[32,2048]{1,0:T(8,128)(2,1)S(1)}, bf16[32,2048]{1,0:T(8,128)(2,1)S(1)}, u32[]{:S(2)}, u32[]{:S(2)}) %collective-permute-start.1) | collective-permute-done | bytes 131104 | tf_op jit(solution)/shard_map/while/body/eval_jaxpr/ppermute | solution.py:12
  425.8 7.2 %conditional.5 = (bf16[32,2048]{1,0:T(8,128)(2,1)S(1)}, bf16[8,32,2048]{2,1,0:T(8,128)(2,1)S(1)}) conditional(s32[]{:T(128)} %convert_element_type.123, bf16[8,32,2048]{2,1,0:T(8,128)(2,1)S(1)} %get-tuple-element.615, (pred[]{:T(512)}, s32[]{:T(128)}, bf16[8,32,2048]{2,1,0:T(8,128)(2,1)}, bf16[32,2048]{1,0:T(8,128)(2,1)S(1)}, ...), branch_computations={%region_8.8_spmd, %region_9.11_spmd} | conditional | flops 269353088 | bytes 10093621 | solution.py:96
  442.0 7.2 %conditional.5 = (bf16[32,2048]{1,0:T(8,128)(2,1)S(1)}, bf16[8,32,2048]{2,1,0:T(8,128)(2,1)S(1)}) conditional(s32[]{:T(128)} %convert_element_type.123, bf16[8,32,2048]{2,1,0:T(8,128)(2,1)S(1)} %get-tuple-element.615, (pred[]{:T(512)}, s32[]{:T(128)}, bf16[8,32,2048]{2,1,0:T(8,128)(2,1)}, bf16[32,2048]{1,0:T(8,128)(2,1)S(1)}, ...), branch_computations={%region_8.8_spmd, %region_9.11_spmd} | conditional | flops 269353088 | bytes 10093621 | solution.py:96
  458.2 7.2 %conditional.5 = (bf16[32,2048]{1,0:T(8,128)(2,1)S(1)}, bf16[8,32,2048]{2,1,0:T(8,128)(2,1)S(1)}) conditional(s32[]{:T(128)} %convert_element_type.123, bf16[8,32,2048]{2,1,0:T(8,128)(2,1)S(1)} %get-tuple-element.615, (pred[]{:T(512)}, s32[]{:T(128)}, bf16[8,32,2048]{2,1,0:T(8,128)(2,1)}, bf16[32,2048]{1,0:T(8,128)(2,1)S(1)}, ...), branch_computations={%region_8.8_spmd, %region_9.11_spmd} | conditional | flops 269353088 | bytes 10093621 | solution.py:96
  474.4 7.2 %conditional.5 = (bf16[32,2048]{1,0:T(8,128)(2,1)S(1)}, bf16[8,32,2048]{2,1,0:T(8,128)(2,1)S(1)}) conditional(s32[]{:T(128)} %convert_element_type.123, bf16[8,32,2048]{2,1,0:T(8,128)(2,1)S(1)} %get-tuple-element.615, (pred[]{:T(512)}, s32[]{:T(128)}, bf16[8,32,2048]{2,1,0:T(8,128)(2,1)}, bf16[32,2048]{1,0:T(8,128)(2,1)S(1)}, ...), branch_computations={%region_8.8_spmd, %region_9.11_spmd} | conditional | flops 269353088 | bytes 10093621 | solution.py:96
  490.7 7.2 %conditional.5 = (bf16[32,2048]{1,0:T(8,128)(2,1)S(1)}, bf16[8,32,2048]{2,1,0:T(8,128)(2,1)S(1)}) conditional(s32[]{:T(128)} %convert_element_type.123, bf16[8,32,2048]{2,1,0:T(8,128)(2,1)S(1)} %get-tuple-element.615, (pred[]{:T(512)}, s32[]{:T(128)}, bf16[8,32,2048]{2,1,0:T(8,128)(2,1)}, bf16[32,2048]{1,0:T(8,128)(2,1)S(1)}, ...), branch_computations={%region_8.8_spmd, %region_9.11_spmd} | conditional | flops 269353088 | bytes 10093621 | solution.py:96
  506.9 7.2 %conditional.5 = (bf16[32,2048]{1,0:T(8,128)(2,1)S(1)}, bf16[8,32,2048]{2,1,0:T(8,128)(2,1)S(1)}) conditional(s32[]{:T(128)} %convert_element_type.123, bf16[8,32,2048]{2,1,0:T(8,128)(2,1)S(1)} %get-tuple-element.615, (pred[]{:T(512)}, s32[]{:T(128)}, bf16[8,32,2048]{2,1,0:T(8,128)(2,1)}, bf16[32,2048]{1,0:T(8,128)(2,1)S(1)}, ...), branch_computations={%region_8.8_spmd, %region_9.11_spmd} | conditional | flops 269353088 | bytes 10093621 | solution.py:96
  526.7 68.0 %reduce-scatter.2.cloned.1.call-done = bf16[512,2048]{1,0:T(8,128)(2,1)} async-done(((bf16[2048,2048]{1,0:T(8,128)(2,1)}), bf16[512,2048]{1,0:T(8,128)(2,1)}) %reduce-scatter.2.cloned.1.call-update) | async-done | bytes 2097168 | tf_op jit(solution)/shard_map/reduce_scatter | solution.py:103
  (218 shorter events, 346.7 us)
Async XLA Ops:
  7.2 63.4 %all-gather.3.cloned.1.call-start = ((), (), s32[]{:S(2)}) async-start(), calls=%async_computation.2 | async-start | bytes 10485760 | tf_op jit(solution)/shard_map/all_gather | solution.py:30
  7.9 586.7 %reduce-scatter.2.cloned.1.call-start = ((), (), s32[]{:S(2)}) async-start(), calls=%async_computation.1 | async-start | bytes 10485760 | tf_op jit(solution)/shard_map/reduce_scatter | solution.py:103
  163.5 7.8 %collective-permute-start = (bf16[32,2048]{1,0:T(8,128)(2,1)S(1)}, bf16[32,2048]{1,0:T(8,128)(2,1)S(1)}, u32[]{:S(2)}, u32[]{:S(2)}) collective-permute-start(bf16[32,2048]{1,0:T(8,128)(2,1)S(1)} %get-tuple-element.538), channel_id=1, source_target_pairs={{0,4},{4,8},{8,12},{12,16},{16,20},{20,24},{24,28},{1,5},{5,9},{9,... | collective-permute-start | bytes 393224 | tf_op jit(solution)/shard_map/while/body/eval_jaxpr/ppermute | solution.py:12
  178.8 7.8 %collective-permute-start = (bf16[32,2048]{1,0:T(8,128)(2,1)S(1)}, bf16[32,2048]{1,0:T(8,128)(2,1)S(1)}, u32[]{:S(2)}, u32[]{:S(2)}) collective-permute-start(bf16[32,2048]{1,0:T(8,128)(2,1)S(1)} %get-tuple-element.538), channel_id=1, source_target_pairs={{0,4},{4,8},{8,12},{12,16},{16,20},{20,24},{24,28},{1,5},{5,9},{9,... | collective-permute-start | bytes 393224 | tf_op jit(solution)/shard_map/while/body/eval_jaxpr/ppermute | solution.py:12
  187.8 14.9 %collective-permute-start = (bf16[32,2048]{1,0:T(8,128)(2,1)S(1)}, bf16[32,2048]{1,0:T(8,128)(2,1)S(1)}, u32[]{:S(2)}, u32[]{:S(2)}) collective-permute-start(bf16[32,2048]{1,0:T(8,128)(2,1)S(1)} %get-tuple-element.538), channel_id=1, source_target_pairs={{0,4},{4,8},{8,12},{12,16},{16,20},{20,24},{24,28},{1,5},{5,9},{9,... | collective-permute-start | bytes 393224 | tf_op jit(solution)/shard_map/while/body/eval_jaxpr/ppermute | solution.py:12
  212.1 14.1 %collective-permute-start = (bf16[32,2048]{1,0:T(8,128)(2,1)S(1)}, bf16[32,2048]{1,0:T(8,128)(2,1)S(1)}, u32[]{:S(2)}, u32[]{:S(2)}) collective-permute-start(bf16[32,2048]{1,0:T(8,128)(2,1)S(1)} %get-tuple-element.538), channel_id=1, source_target_pairs={{0,4},{4,8},{8,12},{12,16},{16,20},{20,24},{24,28},{1,5},{5,9},{9,... | collective-permute-start | bytes 393224 | tf_op jit(solution)/shard_map/while/body/eval_jaxpr/ppermute | solution.py:12
  227.4 8.8 %collective-permute-start = (bf16[32,2048]{1,0:T(8,128)(2,1)S(1)}, bf16[32,2048]{1,0:T(8,128)(2,1)S(1)}, u32[]{:S(2)}, u32[]{:S(2)}) collective-permute-start(bf16[32,2048]{1,0:T(8,128)(2,1)S(1)} %get-tuple-element.538), channel_id=1, source_target_pairs={{0,4},{4,8},{8,12},{12,16},{16,20},{20,24},{24,28},{1,5},{5,9},{9,... | collective-permute-start | bytes 393224 | tf_op jit(solution)/shard_map/while/body/eval_jaxpr/ppermute | solution.py:12
  237.4 8.8 %collective-permute-start = (bf16[32,2048]{1,0:T(8,128)(2,1)S(1)}, bf16[32,2048]{1,0:T(8,128)(2,1)S(1)}, u32[]{:S(2)}, u32[]{:S(2)}) collective-permute-start(bf16[32,2048]{1,0:T(8,128)(2,1)S(1)} %get-tuple-element.538), channel_id=1, source_target_pairs={{0,4},{4,8},{8,12},{12,16},{16,20},{20,24},{24,28},{1,5},{5,9},{9,... | collective-permute-start | bytes 393224 | tf_op jit(solution)/shard_map/while/body/eval_jaxpr/ppermute | solution.py:12
  247.4 8.9 %collective-permute-start = (bf16[32,2048]{1,0:T(8,128)(2,1)S(1)}, bf16[32,2048]{1,0:T(8,128)(2,1)S(1)}, u32[]{:S(2)}, u32[]{:S(2)}) collective-permute-start(bf16[32,2048]{1,0:T(8,128)(2,1)S(1)} %get-tuple-element.538), channel_id=1, source_target_pairs={{0,4},{4,8},{8,12},{12,16},{16,20},{20,24},{24,28},{1,5},{5,9},{9,... | collective-permute-start | bytes 393224 | tf_op jit(solution)/shard_map/while/body/eval_jaxpr/ppermute | solution.py:12
  257.5 9.8 %collective-permute-start = (bf16[32,2048]{1,0:T(8,128)(2,1)S(1)}, bf16[32,2048]{1,0:T(8,128)(2,1)S(1)}, u32[]{:S(2)}, u32[]{:S(2)}) collective-permute-start(bf16[32,2048]{1,0:T(8,128)(2,1)S(1)} %get-tuple-element.538), channel_id=1, source_target_pairs={{0,4},{4,8},{8,12},{12,16},{16,20},{20,24},{24,28},{1,5},{5,9},{9,... | collective-permute-start | bytes 393224 | tf_op jit(solution)/shard_map/while/body/eval_jaxpr/ppermute | solution.py:12
  269.5 8.1 %collective-permute-start.1 = (bf16[32,2048]{1,0:T(8,128)(2,1)S(1)}, bf16[32,2048]{1,0:T(8,128)(2,1)S(1)}, u32[]{:S(2)}, u32[]{:S(2)}) collective-permute-start(bf16[32,2048]{1,0:T(8,128)(2,1)S(1)} %get-tuple-element.550), channel_id=1, source_target_pairs={{4,0},{8,4},{12,8},{16,12},{20,16},{24,20},{28,24},{5,1},{9,5},{13... | collective-permute-start | bytes 393224 | tf_op jit(solution)/shard_map/while/body/eval_jaxpr/ppermute | solution.py:12
  278.9 11.3 %collective-permute-start.1 = (bf16[32,2048]{1,0:T(8,128)(2,1)S(1)}, bf16[32,2048]{1,0:T(8,128)(2,1)S(1)}, u32[]{:S(2)}, u32[]{:S(2)}) collective-permute-start(bf16[32,2048]{1,0:T(8,128)(2,1)S(1)} %get-tuple-element.550), channel_id=1, source_target_pairs={{4,0},{8,4},{12,8},{16,12},{20,16},{24,20},{28,24},{5,1},{9,5},{13... | collective-permute-start | bytes 393224 | tf_op jit(solution)/shard_map/while/body/eval_jaxpr/ppermute | solution.py:12
  291.4 7.8 %collective-permute-start.1 = (bf16[32,2048]{1,0:T(8,128)(2,1)S(1)}, bf16[32,2048]{1,0:T(8,128)(2,1)S(1)}, u32[]{:S(2)}, u32[]{:S(2)}) collective-permute-start(bf16[32,2048]{1,0:T(8,128)(2,1)S(1)} %get-tuple-element.550), channel_id=1, source_target_pairs={{4,0},{8,4},{12,8},{16,12},{20,16},{24,20},{28,24},{5,1},{9,5},{13... | collective-permute-start | bytes 393224 | tf_op jit(solution)/shard_map/while/body/eval_jaxpr/ppermute | solution.py:12
  300.5 11.8 %collective-permute-start.1 = (bf16[32,2048]{1,0:T(8,128)(2,1)S(1)}, bf16[32,2048]{1,0:T(8,128)(2,1)S(1)}, u32[]{:S(2)}, u32[]{:S(2)}) collective-permute-start(bf16[32,2048]{1,0:T(8,128)(2,1)S(1)} %get-tuple-element.550), channel_id=1, source_target_pairs={{4,0},{8,4},{12,8},{16,12},{20,16},{24,20},{28,24},{5,1},{9,5},{13... | collective-permute-start | bytes 393224 | tf_op jit(solution)/shard_map/while/body/eval_jaxpr/ppermute | solution.py:12
  313.6 7.8 %collective-permute-start.1 = (bf16[32,2048]{1,0:T(8,128)(2,1)S(1)}, bf16[32,2048]{1,0:T(8,128)(2,1)S(1)}, u32[]{:S(2)}, u32[]{:S(2)}) collective-permute-start(bf16[32,2048]{1,0:T(8,128)(2,1)S(1)} %get-tuple-element.550), channel_id=1, source_target_pairs={{4,0},{8,4},{12,8},{16,12},{20,16},{24,20},{28,24},{5,1},{9,5},{13... | collective-permute-start | bytes 393224 | tf_op jit(solution)/shard_map/while/body/eval_jaxpr/ppermute | solution.py:12
  322.6 10.7 %collective-permute-start.1 = (bf16[32,2048]{1,0:T(8,128)(2,1)S(1)}, bf16[32,2048]{1,0:T(8,128)(2,1)S(1)}, u32[]{:S(2)}, u32[]{:S(2)}) collective-permute-start(bf16[32,2048]{1,0:T(8,128)(2,1)S(1)} %get-tuple-element.550), channel_id=1, source_target_pairs={{4,0},{8,4},{12,8},{16,12},{20,16},{24,20},{28,24},{5,1},{9,5},{13... | collective-permute-start | bytes 393224 | tf_op jit(solution)/shard_map/while/body/eval_jaxpr/ppermute | solution.py:12
  334.6 57.5 %collective-permute-start.1 = (bf16[32,2048]{1,0:T(8,128)(2,1)S(1)}, bf16[32,2048]{1,0:T(8,128)(2,1)S(1)}, u32[]{:S(2)}, u32[]{:S(2)}) collective-permute-start(bf16[32,2048]{1,0:T(8,128)(2,1)S(1)} %get-tuple-element.550), channel_id=1, source_target_pairs={{4,0},{8,4},{12,8},{16,12},{20,16},{24,20},{28,24},{5,1},{9,5},{13... | collective-permute-start | bytes 393224 | tf_op jit(solution)/shard_map/while/body/eval_jaxpr/ppermute | solution.py:12
  400.6 7.8 %collective-permute-start.1 = (bf16[32,2048]{1,0:T(8,128)(2,1)S(1)}, bf16[32,2048]{1,0:T(8,128)(2,1)S(1)}, u32[]{:S(2)}, u32[]{:S(2)}) collective-permute-start(bf16[32,2048]{1,0:T(8,128)(2,1)S(1)} %get-tuple-element.550), channel_id=1, source_target_pairs={{4,0},{8,4},{12,8},{16,12},{20,16},{24,20},{28,24},{5,1},{9,5},{13... | collective-permute-start | bytes 393224 | tf_op jit(solution)/shard_map/while/body/eval_jaxpr/ppermute | solution.py:12
  416.8 7.8 %collective-permute-start.1 = (bf16[32,2048]{1,0:T(8,128)(2,1)S(1)}, bf16[32,2048]{1,0:T(8,128)(2,1)S(1)}, u32[]{:S(2)}, u32[]{:S(2)}) collective-permute-start(bf16[32,2048]{1,0:T(8,128)(2,1)S(1)} %get-tuple-element.550), channel_id=1, source_target_pairs={{4,0},{8,4},{12,8},{16,12},{20,16},{24,20},{28,24},{5,1},{9,5},{13... | collective-permute-start | bytes 393224 | tf_op jit(solution)/shard_map/while/body/eval_jaxpr/ppermute | solution.py:12
  433.0 7.8 %collective-permute-start.1 = (bf16[32,2048]{1,0:T(8,128)(2,1)S(1)}, bf16[32,2048]{1,0:T(8,128)(2,1)S(1)}, u32[]{:S(2)}, u32[]{:S(2)}) collective-permute-start(bf16[32,2048]{1,0:T(8,128)(2,1)S(1)} %get-tuple-element.550), channel_id=1, source_target_pairs={{4,0},{8,4},{12,8},{16,12},{20,16},{24,20},{28,24},{5,1},{9,5},{13... | collective-permute-start | bytes 393224 | tf_op jit(solution)/shard_map/while/body/eval_jaxpr/ppermute | solution.py:12
  449.2 7.8 %collective-permute-start.1 = (bf16[32,2048]{1,0:T(8,128)(2,1)S(1)}, bf16[32,2048]{1,0:T(8,128)(2,1)S(1)}, u32[]{:S(2)}, u32[]{:S(2)}) collective-permute-start(bf16[32,2048]{1,0:T(8,128)(2,1)S(1)} %get-tuple-element.550), channel_id=1, source_target_pairs={{4,0},{8,4},{12,8},{16,12},{20,16},{24,20},{28,24},{5,1},{9,5},{13... | collective-permute-start | bytes 393224 | tf_op jit(solution)/shard_map/while/body/eval_jaxpr/ppermute | solution.py:12
  465.4 7.8 %collective-permute-start.1 = (bf16[32,2048]{1,0:T(8,128)(2,1)S(1)}, bf16[32,2048]{1,0:T(8,128)(2,1)S(1)}, u32[]{:S(2)}, u32[]{:S(2)}) collective-permute-start(bf16[32,2048]{1,0:T(8,128)(2,1)S(1)} %get-tuple-element.550), channel_id=1, source_target_pairs={{4,0},{8,4},{12,8},{16,12},{20,16},{24,20},{28,24},{5,1},{9,5},{13... | collective-permute-start | bytes 393224 | tf_op jit(solution)/shard_map/while/body/eval_jaxpr/ppermute | solution.py:12
  481.7 7.8 %collective-permute-start.1 = (bf16[32,2048]{1,0:T(8,128)(2,1)S(1)}, bf16[32,2048]{1,0:T(8,128)(2,1)S(1)}, u32[]{:S(2)}, u32[]{:S(2)}) collective-permute-start(bf16[32,2048]{1,0:T(8,128)(2,1)S(1)} %get-tuple-element.550), channel_id=1, source_target_pairs={{4,0},{8,4},{12,8},{16,12},{20,16},{24,20},{28,24},{5,1},{9,5},{13... | collective-permute-start | bytes 393224 | tf_op jit(solution)/shard_map/while/body/eval_jaxpr/ppermute | solution.py:12
  497.9 7.8 %collective-permute-start.1 = (bf16[32,2048]{1,0:T(8,128)(2,1)S(1)}, bf16[32,2048]{1,0:T(8,128)(2,1)S(1)}, u32[]{:S(2)}, u32[]{:S(2)}) collective-permute-start(bf16[32,2048]{1,0:T(8,128)(2,1)S(1)} %get-tuple-element.550), channel_id=1, source_target_pairs={{4,0},{8,4},{12,8},{16,12},{20,16},{24,20},{28,24},{5,1},{9,5},{13... | collective-permute-start | bytes 393224 | tf_op jit(solution)/shard_map/while/body/eval_jaxpr/ppermute | solution.py:12
  (10 other events, 58.9 us)
Sparse Core Ops, SparseCore 0:
  9.6 60.9 all-gather.2
  526.8 67.7 reduce-scatter.1
where the time goes:
time: 608 us; the launch traced here: 606 us
  waiting for transfers between devices  324 us (53%)
  starting transfers between devices  107 us (18%)
  matrix products  95 us (16%)
  other arithmetic  23.9 us (4%)
  local copies, waits for them, and re-layouts  21.4 us (4%)
  loops' own time  20.3 us (3%)
  between operations  14.1 us (2%)
    ppermute x30, waiting for transfers between devices, from_behind(): lax.ppermute(value, axis, [(source, source + steps) for source in range(l...  196 us
    ppermute x30, starting transfers between devices, from_behind(): lax.ppermute(value, axis, [(source, source + steps) for source in range(l...  107 us
    reduce_scatter x1, waiting for transfers between devices, local(): lax.psum_scatter(lax.dot_general(normed_all, cot_all, (((0,), (0,)), ((),...  68 us
    all_gather x1, waiting for transfers between devices, local(): weight = lax.all_gather(layer_weight[0], 'dp', axis=0, tiled=True)  59 us
    dot_general x8, matrix products, run_back(): lax.dot_general(incoming, weight, (((1,), (1,)), ((), ())), preferred_ele...  48.5 us
    dot_general x8, matrix products, run_layer(): jnp.dot(normed, weight, preferred_element_type=jnp.float32)  40.8 us
    dynamic_slice x30, local copies, waits for them, and re-layouts, local(): lax.scan(forward_step, (blank, storage, storage), steps_total)  17.5 us
  transfers between devices with their start and end apart: 32, of which 32 were waited for; matrix products, arithmetic and copies ran while one was open for 1% of the time, Pallas kernels for 0%

commit v1 on v0

v1 whole, which is shorter than its diff:
```python
import functools

import jax
import jax.numpy as jnp
from jax import lax
from jax.experimental import pallas as pl
from jax.experimental.pallas import tpu as pltpu
from jax.sharding import PartitionSpec as P

epsilon = 1e-05
CHUNKS = 4
TILE = 512


def relay_kernel(sections, replicas, blocks, base_ref, stream_ref, weight_ref, top_ref,
                 decoded_ref, normed_all, cot_all,
                 weight, rows_in, normed, cot_in, cot_out, product,
                 load_sem, w_send, w_recv, w_side_send, w_side_recv,
                 x_send, x_recv, g_send, g_recv, n_send, n_recv,
                 c_send, c_recv, c_side_send, c_side_recv, own_sem):
    s = lax.axis_index("section")
    me = lax.axis_index("dp")
    last = sections - 1
    chips = replicas // 2
    chip, core = me // 2, lax.rem(me, 2)
    sibling = chip * 2 + 1 - core
    total, width = rows_in.shape
    step_rows = total // blocks
    shard = weight_ref.shape[0]
    piece = shard // CHUNKS
    after, before = lax.rem(s + 1, sections), lax.rem(s + last, sections)

    def peer(offset):
        return lax.rem(chip + offset, chips) * 2 + core

    def source(offset):
        return lax.rem(chip + chips - offset, chips) * 2

    def block(m):
        return pl.ds(pl.multiple_of(m * step_rows, step_rows), step_rows)

    def remote(src, dst, send, recv, **where):
        return pltpu.make_async_remote_copy(
            src_ref=src, dst_ref=dst, send_sem=send, recv_sem=recv,
            device_id=where, device_id_type=pl.DeviceIdType.MESH)

    barrier = pltpu.get_barrier_semaphore()

    def greet(**where):
        pl.semaphore_signal(barrier, inc=1, device_id=where, device_id_type=pl.DeviceIdType.MESH)

    for offset in range(1, replicas):
        greet(dp=lax.rem(me + offset, replicas))

    @pl.when(s < last)
    def _():
        greet(section=after)

    @pl.when(s > 0)
    def _():
        greet(section=before)

    stream_load = pltpu.make_async_copy(stream_ref, rows_in, load_sem.at[0])
    top_load = pltpu.make_async_copy(top_ref, cot_in, load_sem.at[1])
    shard_load = pltpu.make_async_copy(
        weight_ref, weight.at[pl.ds(pl.multiple_of(me * shard, shard), shard)], load_sem.at[2])
    shard_load.start()

    @pl.when(s == 0)
    def _():
        stream_load.start()

    @pl.when(s == last)
    def _():
        top_load.start()

    pl.semaphore_wait(
        barrier, replicas - 1 + jnp.minimum(s, 1) + jnp.minimum(last - s, 1))

    def weight_rows(owner, q):
        return weight.at[pl.ds(pl.multiple_of(owner * shard + q * piece, piece), piece)]

    def weight_direct(offset, q):
        return remote(weight_ref.at[pl.ds(q * piece, piece)], weight_rows(me, q),
                      w_send.at[offset - 1, q], w_recv.at[offset - 1, q], dp=peer(offset))

    def weight_side(offset, q):
        if offset == 0:
            src = weight_ref.at[pl.ds(q * piece, piece)]
        else:
            src = weight_rows(source(offset) + core, q)
        return remote(src, weight_rows(source(offset) + core, q),
                      w_side_send.at[offset, q], w_side_recv.at[offset, q], dp=sibling)

    for q in range(CHUNKS):
        for offset in range(1, chips):
            weight_direct(offset, q).start()
        weight_side(0, q).start()
    for q in range(CHUNKS):
        for offset in range(1, chips):
            weight_direct(offset, q).wait_recv()
            weight_side(offset, q).start()
    shard_load.wait()
    for q in range(CHUNKS):
        for offset in range(chips):
            weight_side(offset, q).wait_recv()

    @pl.when(s == 0)
    def _():
        stream_load.wait()

    @pl.when(s == last)
    def _():
        top_load.wait()

    def send_rows(m):
        return remote(decoded_ref.at[block(m)], rows_in.at[block(m)],
                      x_send.at[m], x_recv.at[m], section=after)

    def send_cot(m):
        return remote(cot_out.at[block(m)], cot_in.at[block(m)],
                      g_send.at[m], g_recv.at[m], section=before)

    def send_normed(offset):
        other = lax.rem(me + offset, replicas)
        return remote(normed.at[:, pl.ds(pl.multiple_of(other * shard, shard), shard)],
                      normed_all.at[pl.ds(pl.multiple_of(me * total, total), total)],
                      n_send.at[offset - 1], n_recv.at[offset - 1], dp=other)

    own_normed = pltpu.make_async_copy(
        normed.at[:, pl.ds(pl.multiple_of(me * shard, shard), shard)],
        normed_all.at[pl.ds(pl.multiple_of(me * total, total), total)], load_sem.at[3])

    def cot_rows(owner, m):
        return cot_all.at[pl.ds(pl.multiple_of(owner * total + m * step_rows, step_rows), step_rows)]

    def cot_direct(offset, m):
        return remote(cot_in.at[block(m)], cot_rows(me, m),
                      c_send.at[offset - 1, m], c_recv.at[offset - 1, m], dp=peer(offset))

    def cot_side(offset, m):
        owner = source(offset) + core
        src = cot_in.at[block(m)] if offset == 0 else cot_rows(owner, m)
        return remote(src, cot_rows(owner, m),
                      c_side_send.at[offset, m], c_side_recv.at[offset, m], dp=sibling)

    def cot_own(m):
        return pltpu.make_async_copy(cot_in.at[block(m)], cot_rows(me, m), own_sem.at[m])

    def relay(m):
        for offset in range(1, chips):
            cot_direct(offset, m).wait_recv()
            cot_side(offset, m).start()

    def forward(m):
        @pl.when(s > 0)
        def _():
            send_rows(m).wait_recv()

        values = rows_in[block(m), :].astype(jnp.float32)
        scale = lax.rsqrt(jnp.mean(values * values, axis=-1, keepdims=True) + epsilon)
        scaled = (values * scale).astype(jnp.bfloat16)
        normed[block(m), :] = scaled
        squares = jnp.zeros((step_rows, 1), jnp.float32)
        for start in range(0, width, TILE):
            part = rows_in[block(m), start:start + TILE].astype(jnp.float32) + jnp.dot(
                scaled, weight[:, start:start + TILE], preferred_element_type=jnp.float32)
            product[:, start:start + TILE] = part
            squares += jnp.sum(part * part, axis=-1, keepdims=True)
        bound = 2.0 * jnp.sqrt(squares / width + epsilon)
        base = base_ref[block(m), :].astype(jnp.float32)
        delta = jnp.clip(product[...] - base, -bound, bound).astype(jnp.bfloat16)
        decoded_ref[block(m), :] = (base + delta.astype(jnp.float32)).astype(jnp.bfloat16)

        @pl.when(s < last)
        def _():
            send_rows(m).start()

    def backward(m):
        @pl.when(s < last)
        def _():
            send_cot(m).wait_recv()

        cot_side(0, m).start()
        for offset in range(1, chips):
            cot_direct(offset, m).start()
        cot_own(m).start()

        @pl.when(s > 0)
        def _():
            values = rows_in[block(m), :].astype(jnp.float32)
            scale = lax.rsqrt(jnp.mean(values * values, axis=-1, keepdims=True) + epsilon)
            incoming = cot_in[block(m), :]
            along = jnp.zeros((step_rows, 1), jnp.float32)
            for start in range(0, width, TILE):
                part = lax.dot_general(incoming, weight[start:start + TILE, :],
                                       (((1,), (1,)), ((), ())), preferred_element_type=jnp.float32)
                product[:, start:start + TILE] = part
                along += jnp.sum(
                    part * rows_in[block(m), start:start + TILE].astype(jnp.float32),
                    axis=-1, keepdims=True)
            through = scale * (product[...] - values * (scale * scale * (along / width)))
            cot_out[block(m), :] = (incoming.astype(jnp.float32) + through).astype(jnp.bfloat16)
            send_cot(m).start()

        @pl.when(m > 0)
        def _():
            relay(m - 1)

    lag = jnp.minimum(blocks, ((last - s) * 5) // 2)

    def step(k, carry):
        @pl.when(k < blocks)
        def _():
            forward(k)

        @pl.when(k == blocks - 1)
        def _():
            own_normed.start()
            for offset in range(1, replicas):
                send_normed(offset).start()

        @pl.when((k >= lag) & (k < lag + blocks))
        def _():
            backward(k - lag)

        return carry

    lax.fori_loop(0, 2 * blocks, step, 0)
    relay(blocks - 1)

    own_normed.wait()
    for offset in range(1, replicas):
        send_normed(offset).wait_send()
        send_normed(offset).wait_recv()
    for q in range(CHUNKS):
        for offset in range(1, chips):
            weight_direct(offset, q).wait_send()
        for offset in range(chips):
            weight_side(offset, q).wait_send()

    def finish(m, carry):
        @pl.when(s < last)
        def _():
            send_rows(m).wait_send()

        @pl.when(s > 0)
        def _():
            send_cot(m).wait_send()

        cot_own(m).wait()
        for offset in range(1, chips):
            cot_direct(offset, m).wait_send()
        for offset in range(chips):
            cot_side(offset, m).wait_send()
            cot_side(offset, m).wait_recv()
        return carry

    lax.fori_loop(0, blocks, finish, 0)


def local(sections, replicas, stream_in, sample_ids, epoch_buffer, layer_weight, top_cotangent):
    total, width = stream_in.shape
    blocks = sample_ids.shape[1]
    shard = layer_weight.shape[1]
    chips = replicas // 2
    base = jnp.take(epoch_buffer[0], sample_ids[0], axis=0, mode="clip").reshape(total, width)
    dma = pltpu.SemaphoreType.DMA
    vmem = pl.BlockSpec(memory_space=pltpu.VMEM)
    anywhere = pl.BlockSpec(memory_space=pl.ANY)
    far = max(chips - 1, 1)
    decoded, normed_all, cot_all = pl.pallas_call(
        functools.partial(relay_kernel, sections, replicas, blocks),
        out_shape=(
            jax.ShapeDtypeStruct((total, width), jnp.bfloat16),
            jax.ShapeDtypeStruct((replicas * total, shard), jnp.bfloat16),
            jax.ShapeDtypeStruct((replicas * total, width), jnp.bfloat16),
        ),
        in_specs=[vmem, anywhere, anywhere, anywhere],
        out_specs=(vmem, anywhere, anywhere),
        scratch_shapes=[
            pltpu.VMEM((width, width), jnp.bfloat16),
            pltpu.VMEM((total, width), jnp.bfloat16),
            pltpu.VMEM((total, width), jnp.bfloat16),
            pltpu.VMEM((total, width), jnp.bfloat16),
            pltpu.VMEM((total, width), jnp.bfloat16),
            pltpu.VMEM((total // blocks, width), jnp.float32),
            dma((4,)),
            dma((far, CHUNKS)), dma((far, CHUNKS)), dma((chips, CHUNKS)), dma((chips, CHUNKS)),
            dma((blocks,)), dma((blocks,)), dma((blocks,)), dma((blocks,)),
            dma((replicas - 1,)), dma((replicas - 1,)),
            dma((far, blocks)), dma((far, blocks)), dma((chips, blocks)), dma((chips, blocks)),
            dma((blocks,)),
        ],
        compiler_params=pltpu.CompilerParams(
            collective_id=0, has_side_effects=True, vmem_limit_bytes=48 * 1024 * 1024),
    )(base, stream_in, layer_weight[0], top_cotangent)
    gradient = lax.dot_general(
        normed_all, cot_all, (((0,), (0,)), ((), ())), preferred_element_type=jnp.float32)
    return (decoded[None], gradient[None])


def solution(mesh):
    in_specs = (
        P("dp", None),
        P("dp", None),
        P("section", "dp", None, None),
        P("section", "dp", None),
        P("dp", None),
    )
    out_specs = (P("section", "dp", None), P("section", "dp", None))
    body = functools.partial(local, mesh.shape["section"], mesh.shape["dp"])
    return jax.shard_map(body, mesh=mesh, in_specs=in_specs, out_specs=out_specs, check_vma=False)
```

time: 608 us -> 216 us (0.36)
  waiting for transfers between devices: 324 us -> 0 us
  Pallas kernels: 0 us -> 202 us
  starting transfers between devices: 107 us -> 0 us
  matrix products: 95 us -> 6.58 us
  other arithmetic: 23.9 us -> 0.66 us
  loops' own time: 20.3 us -> 0 us
  local copies, waits for them, and re-layouts: 21.4 us -> 6.21 us
  between operations: 14.1 us -> 0.66 us
    pallas_call x0 -> x1, Pallas kernels: none -> 202 us  [local(): pl.pallas_call(functools.partial(relay_kernel, sections, replicas, blocks...]
    ppermute x30 -> x0, waiting for transfers between devices: 196 us -> none  [from_behind(): lax.ppermute(value, axis, [(source, source + steps) for source in range(l...]
    ppermute x30 -> x0, starting transfers between devices: 107 us -> none  [from_behind(): lax.ppermute(value, axis, [(source, source + steps) for source in range(l...]
    dot_general x16 -> x0, matrix products: 89.3 us -> none  [the longest x8 48.5 us: run_back(): lax.dot_general(incoming, weight, (((1,), (1,)), ((), ())), preferred_ele...]
    reduce_scatter x1 -> x0, waiting for transfers between devices: 68 us -> none  [local(): lax.psum_scatter(lax.dot_general(normed_all, cot_all, (((0,), (0,)), ((),...]
    all_gather x1 -> x0, waiting for transfers between devices: 59 us -> none  [local(): weight = lax.all_gather(layer_weight[0], 'dp', axis=0, tiled=True)]
    another operation x32 -> x0, loops' own time: 20.3 us -> none  [the longest x1 10.2 us: local(): lax.scan(backward_step, (blank, storage), steps_total)]
    dynamic_slice x30 -> x0, local copies, waits for them, and re-layouts: 17.5 us -> none  [local(): lax.scan(forward_step, (blank, storage, storage), steps_total)]
  transfers between devices with their start and end apart: 32 -> 0, of which waited for: 32 -> 0; matrix products, arithmetic and copies ran while one was open for 1% -> 0% of each run, Pallas kernels for 0% -> 0%
where the time goes in v1:
time: 216 us
  Pallas kernels  202 us (94%)
  matrix products  6.58 us (3%)
  local copies, waits for them, and re-layouts  6.21 us (3%)
    pallas_call x1, Pallas kernels, local(): pl.pallas_call(functools.partial(relay_kernel, sections, replicas, blocks...  202 us
    dot_general x1, matrix products, local(): lax.dot_general(normed_all, cot_all, (((0,), (0,)), ((), ())), preferred_...  6.58 us

profile of v1, /device:TPU:0, one launch (start us, length us, event | category | flops | bytes accessed | tf_op | source)
XLA Modules:
  0.0 216.0 jit_solution(14207574762544391322)
XLA Ops:
  0.6 0.7 pad_clamp_fusion
  1.3 2.8 %gather_fusion = bf16[8,32,2048]{2,1,0:T(8,128)(2,1)S(1)} fusion(bf16[32,32,2048]{2,1,0:T(8,128)(2,1)} %bitcast.12, s32[1024]{0:T(1024)S(1)} %pad_clamp_fusion), kind=kCustom, calls=%fused_computation | custom fusion | bytes 2097184 | tf_op jit(solution)/shard_map/jit(_take)/gather | solution.py:267
  4.1 0.0 copy-start
  4.1 1.2 copy-done
  5.3 0.0 copy-start.1
  5.3 1.2 copy-done.1
  6.6 201.9 %shard_map.68 = (bf16[256,2048]{1,0:T(8,128)(2,1)S(1)}, bf16[1024,512]{1,0:T(8,128)(2,1)S(1)}, bf16[1024,2048]{1,0:T(8,128)(2,1)}) custom-call(bf16[256,2048]{1,0:T(8,128)(2,1)S(1)} %bitcast.9, bf16[256,2048]{1,0:T(8,128)(2,1)S(1)} %copy-done, bf16[512,2048]{1,0:T(8,128)(2,1)} %bitcast.11, bf16[256,2048]{1,0:T(8,128)(2,1)S(1)} %copy-done.1), custom_call_target="tpu_custom_call" | custom-call | tf_op jit(solution)/shard_map/pallas_call | solution.py:272
  208.5 6.6 %convolution_bitcast_fusion = f32[1,512,2048]{2,1,0:T(8,128)} fusion(bf16[1024,512]{1,0:T(8,128)(2,1)S(1)} %get-tuple-element.6, bf16[1024,2048]{1,0:T(8,128)(2,1)} %get-tuple-element.7), kind=kOutput, calls=%fused_computation.1 | convolution fusion | flops 2147483648 | bytes 9437184 | tf_op jit(solution)/shard_map/dot_general | solution.py:298
  215.1 1.0 copy.8
Async XLA Ops:
  4.1 1.2 copy-start
  5.3 1.2 copy-start.1

commit v2 on v1

--- a/solution.py
+++ b/solution.py
@@ -10,11 +10,12 @@
 epsilon = 1e-05
 CHUNKS = 4
 TILE = 512
-
-
-def relay_kernel(sections, replicas, blocks, base_ref, stream_ref, weight_ref, top_ref,
+PIECES = 4
+
+
+def relay_kernel(sections, replicas, blocks, ids_ref, epoch_ref, stream_ref, weight_whole, top_ref,
                  decoded_ref, normed_all, cot_all,
-                 weight, rows_in, normed, cot_in, cot_out, product,
+                 weight, rows_in, normed, cot_in, cot_out, product, ahead, epoch,
                  load_sem, w_send, w_recv, w_side_send, w_side_recv,
                  x_send, x_recv, g_send, g_recv, n_send, n_recv,
                  c_send, c_recv, c_side_send, c_side_recv, own_sem):
@@ -26,7 +27,9 @@
     sibling = chip * 2 + 1 - core
     total, width = rows_in.shape
     step_rows = total // blocks
+    weight_ref = weight_whole.at[0]
     shard = weight_ref.shape[0]
+    span = width // PIECES
     piece = shard // CHUNKS
     after, before = lax.rem(s + 1, sections), lax.rem(s + last, sections)
 
@@ -65,6 +68,7 @@
     shard_load = pltpu.make_async_copy(
         weight_ref, weight.at[pl.ds(pl.multiple_of(me * shard, shard), shard)], load_sem.at[2])
     shard_load.start()
+    epoch_load = pltpu.make_async_copy(epoch_ref.at[0], epoch, load_sem.at[4])
 
     @pl.when(s == 0)
     def _():
@@ -96,6 +100,7 @@
         for offset in range(1, chips):
             weight_direct(offset, q).start()
         weight_side(0, q).start()
+    epoch_load.start()
     for q in range(CHUNKS):
         for offset in range(1, chips):
             weight_direct(offset, q).wait_recv()
@@ -113,13 +118,18 @@
     def _():
         top_load.wait()
 
-    def send_rows(m):
-        return remote(decoded_ref.at[block(m)], rows_in.at[block(m)],
-                      x_send.at[m], x_recv.at[m], section=after)
-
-    def send_cot(m):
-        return remote(cot_out.at[block(m)], cot_in.at[block(m)],
-                      g_send.at[m], g_recv.at[m], section=before)
+    epoch_load.wait()
+
+    def columns(p):
+        return slice(p * span, (p + 1) * span)
+
+    def send_rows(m, p):
+        return remote(decoded_ref.at[block(m), columns(p)], rows_in.at[block(m), columns(p)],
+                      x_send.at[m, p], x_recv.at[m, p], section=after)
+
+    def send_cot(m, p):
+        return remote(cot_out.at[block(m), columns(p)], cot_in.at[block(m), columns(p)],
+                      g_send.at[m, p], g_recv.at[m, p], section=before)
 
     def send_normed(offset):
         other = lax.rem(me + offset, replicas)
@@ -152,62 +162,101 @@
             cot_direct(offset, m).wait_recv()
             cot_side(offset, m).start()
 
+    def squared(m):
+        total_squares = jnp.zeros((step_rows, 1), jnp.float32)
+        for p in range(PIECES):
+            part = rows_in[block(m), columns(p)].astype(jnp.float32)
+            total_squares += jnp.sum(part * part, axis=-1, keepdims=True)
+        return lax.rsqrt(total_squares / width + epsilon)
+
     def forward(m):
-        @pl.when(s > 0)
-        def _():
-            send_rows(m).wait_recv()
-
-        values = rows_in[block(m), :].astype(jnp.float32)
-        scale = lax.rsqrt(jnp.mean(values * values, axis=-1, keepdims=True) + epsilon)
-        scaled = (values * scale).astype(jnp.bfloat16)
-        normed[block(m), :] = scaled
+        for p in range(PIECES):
+            @pl.when(s > 0)
+            def _():
+                send_rows(m, p).wait_recv()
+
+            piece_rows = rows_in[block(m), columns(p)]
+            for start in range(0, width, TILE):
+                part = jnp.dot(piece_rows, weight[columns(p), start:start + TILE],
+                               preferred_element_type=jnp.float32)
+                if p > 0:
+                    part += product[block(m), start:start + TILE]
+                product[block(m), start:start + TILE] = part
+        scale = squared(m)
         squares = jnp.zeros((step_rows, 1), jnp.float32)
-        for start in range(0, width, TILE):
-            part = rows_in[block(m), start:start + TILE].astype(jnp.float32) + jnp.dot(
-                scaled, weight[:, start:start + TILE], preferred_element_type=jnp.float32)
-            product[:, start:start + TILE] = part
+        for p in range(PIECES):
+            values = rows_in[block(m), columns(p)].astype(jnp.float32)
+            part = values + scale * product[block(m), columns(p)]
+            product[block(m), columns(p)] = part
             squares += jnp.sum(part * part, axis=-1, keepdims=True)
         bound = 2.0 * jnp.sqrt(squares / width + epsilon)
-        base = base_ref[block(m), :].astype(jnp.float32)
-        delta = jnp.clip(product[...] - base, -bound, bound).astype(jnp.bfloat16)
-        decoded_ref[block(m), :] = (base + delta.astype(jnp.float32)).astype(jnp.bfloat16)
-
-        @pl.when(s < last)
-        def _():
-            send_rows(m).start()
+        entry = ids_ref[0, m]
+        for p in range(PIECES):
+            base = epoch[entry, :, columns(p)].astype(jnp.float32)
+            delta = jnp.clip(product[block(m), columns(p)] - base, -bound, bound).astype(jnp.bfloat16)
+            decoded_ref[block(m), columns(p)] = (
+                base + delta.astype(jnp.float32)).astype(jnp.bfloat16)
+
+            @pl.when(s < last)
+            def _():
+                send_rows(m, p).start()
+
+        for p in range(PIECES):
+            values = rows_in[block(m), columns(p)].astype(jnp.float32)
+            normed[block(m), columns(p)] = (values * scale).astype(jnp.bfloat16)
+
+    def back_product(m, wait):
+        for p in range(PIECES):
+            if wait:
+                send_cot(m, p).wait_recv()
+            incoming = cot_in[block(m), columns(p)]
+            for start in range(0, width, TILE):
+                part = lax.dot_general(incoming, weight[start:start + TILE, columns(p)],
+                                       (((1,), (1,)), ((), ())), preferred_element_type=jnp.float32)
+                if p > 0:
+                    part += ahead[block(m), start:start + TILE]
+                ahead[block(m), start:start + TILE] = part
 
     def backward(m):
-        @pl.when(s < last)
-        def _():
-            send_cot(m).wait_recv()
+        @pl.when((s < last) & (s > 0))
+        def _():
+            back_product(m, True)
+
+        @pl.when(s == 0)
+        def _():
+            for p in range(PIECES):
+                send_cot(m, p).wait_recv()
+
+        @pl.when(s > 0)
+        def _():
+            scale = squared(m)
+            along = jnp.zeros((step_rows, 1), jnp.float32)
+            for p in range(PIECES):
+                along += jnp.sum(
+                    ahead[block(m), columns(p)] * rows_in[block(m), columns(p)].astype(jnp.float32),
+                    axis=-1, keepdims=True)
+            pull = scale * scale * (along / width)
+            for p in range(PIECES):
+                values = rows_in[block(m), columns(p)].astype(jnp.float32)
+                through = scale * (ahead[block(m), columns(p)] - values * pull)
+                cot_out[block(m), columns(p)] = (
+                    cot_in[block(m), columns(p)].astype(jnp.float32) + through).astype(jnp.bfloat16)
+                send_cot(m, p).start()
 
         cot_side(0, m).start()
         for offset in range(1, chips):
             cot_direct(offset, m).start()
         cot_own(m).start()
 
-        @pl.when(s > 0)
-        def _():
-            values = rows_in[block(m), :].astype(jnp.float32)
-            scale = lax.rsqrt(jnp.mean(values * values, axis=-1, keepdims=True) + epsilon)
-            incoming = cot_in[block(m), :]
-            along = jnp.zeros((step_rows, 1), jnp.float32)
-            for start in range(0, width, TILE):
-                part = lax.dot_general(incoming, weight[start:start + TILE, :],
-                                       (((1,), (1,)), ((), ())), preferred_element_type=jnp.float32)
-                product[:, start:start + TILE] = part
-                along += jnp.sum(
-                    part * rows_in[block(m), start:start + TILE].astype(jnp.float32),
-                    axis=-1, keepdims=True)
-            through = scale * (product[...] - values * (scale * scale * (along / width)))
-            cot_out[block(m), :] = (incoming.astype(jnp.float32) + through).astype(jnp.bfloat16)
-            send_cot(m).start()
-
         @pl.when(m > 0)
         def _():
             relay(m - 1)
 
-    lag = jnp.minimum(blocks, ((last - s) * 5) // 2)
+    @pl.when(s == last)
+    def _():
+        lax.fori_loop(0, blocks, lambda m, carry: (back_product(m, False), carry)[1], 0)
+
+    lag = jnp.minimum(blocks, (last - s) * 3)
 
     def step(k, carry):
         @pl.when(k < blocks)
@@ -242,11 +291,13 @@
     def finish(m, carry):
         @pl.when(s < last)
         def _():
-            send_rows(m).wait_send()
+            for p in range(PIECES):
+                send_rows(m, p).wait_send()
 
         @pl.when(s > 0)
         def _():
-            send_cot(m).wait_send()
+            for p in range(PIECES):
+                send_cot(m, p).wait_send()
 
         cot_own(m).wait()
         for offset in range(1, chips):
@@ -264,7 +315,6 @@
     blocks = sample_ids.shape[1]
     shard = layer_weight.shape[1]
     chips = replicas // 2
-    base = jnp.take(epoch_buffer[0], sample_ids[0], axis=0, mode="clip").reshape(total, width)
     dma = pltpu.SemaphoreType.DMA
     vmem = pl.BlockSpec(memory_space=pltpu.VMEM)
     anywhere = pl.BlockSpec(memory_space=pl.ANY)
@@ -276,7 +326,7 @@
             jax.ShapeDtypeStruct((replicas * total, shard), jnp.bfloat16),
             jax.ShapeDtypeStruct((replicas * total, width), jnp.bfloat16),
         ),
-        in_specs=[vmem, anywhere, anywhere, anywhere],
+        in_specs=[pl.BlockSpec(memory_space=pltpu.SMEM)] + [anywhere] * 4,
         out_specs=(vmem, anywhere, anywhere),
         scratch_shapes=[
             pltpu.VMEM((width, width), jnp.bfloat16),
@@ -284,17 +334,19 @@
             pltpu.VMEM((total, width), jnp.bfloat16),
             pltpu.VMEM((total, width), jnp.bfloat16),
             pltpu.VMEM((total, width), jnp.bfloat16),
-            pltpu.VMEM((total // blocks, width), jnp.float32),
-            dma((4,)),
+            pltpu.VMEM((total, width), jnp.float32),
+            pltpu.VMEM((total, width), jnp.float32),
+            pltpu.VMEM(epoch_buffer.shape[1:], jnp.bfloat16),
+            dma((5,)),
             dma((far, CHUNKS)), dma((far, CHUNKS)), dma((chips, CHUNKS)), dma((chips, CHUNKS)),
-            dma((blocks,)), dma((blocks,)), dma((blocks,)), dma((blocks,)),
+            dma((blocks, PIECES)), dma((blocks, PIECES)), dma((blocks, PIECES)), dma((blocks, PIECES)),
             dma((replicas - 1,)), dma((replicas - 1,)),
             dma((far, blocks)), dma((far, blocks)), dma((chips, blocks)), dma((chips, blocks)),
             dma((blocks,)),
         ],
         compiler_params=pltpu.CompilerParams(
-            collective_id=0, has_side_effects=True, vmem_limit_bytes=48 * 1024 * 1024),
-    )(base, stream_in, layer_weight[0], top_cotangent)
+            collective_id=0, has_side_effects=True, vmem_limit_bytes=60 * 1024 * 1024),
+    )(sample_ids, epoch_buffer, stream_in, layer_weight, top_cotangent)
     gradient = lax.dot_general(
         normed_all, cot_all, (((0,), (0,)), ((), ())), preferred_element_type=jnp.float32)
     return (decoded[None], gradient[None])

time: 216 us -> 196 us (0.907)
  Pallas kernels: 202 us -> 188 us
  local copies, waits for them, and re-layouts: 6.21 us -> 0.97 us
    pallas_call x1, Pallas kernels: 202 us -> 188 us  [local(): pl.pallas_call(functools.partial(relay_kernel, sections, replicas, blocks...]
    gather x1 -> x0, local copies, waits for them, and re-layouts: 2.8 us -> none  [local(): jnp.take(epoch_buffer[0], sample_ids[0], axis=0, mode='clip')]
    unnamed x5 -> x3, local copies, waits for them, and re-layouts: 3.41 us -> 0.97 us
where the time goes in v2:
time: 196 us
  Pallas kernels  188 us (96%)
  matrix products  6.98 us (4%)
    pallas_call x1, Pallas kernels, local(): pl.pallas_call(functools.partial(relay_kernel, sections, replicas, blocks...  188 us
    dot_general x1, matrix products, local(): lax.dot_general(normed_all, cot_all, (((0,), (0,)), ((), ())), preferred_...  6.98 us

profile of v2, /device:TPU:0, one launch (start us, length us, event | category | flops | bytes accessed | tf_op | source)
XLA Modules:
  0.0 196.2 jit_solution(18259631353923366618)
XLA Ops:
  0.6 187.6 %shard_map.68 = (bf16[256,2048]{1,0:T(8,128)(2,1)}, bf16[1024,512]{1,0:T(8,128)(2,1)}, bf16[1024,2048]{1,0:T(8,128)(2,1)}) custom-call(s32[1,8]{1,0:T(1,128)} %ids_ref.1, bf16[1,32,32,2048]{3,2,1,0:T(8,128)(2,1)} %epoch_ref.1, bf16[256,2048]{1,0:T(8,128)(2,1)} %stream_ref.1, bf16[1,512,2048]{2,1,0:T(8,128)(2,1)} %weight_whole.1, bf16[256,2048]{1,0:T(8,128)(2,1)} %top_ref.1), custom_call_target="tpu_custom_call" | custom-call | tf_op jit(solution)/shard_map/pallas_call | solution.py:322
  188.3 0.0 copy-start
  188.3 7.0 %convolution_bitcast_fusion = f32[1,512,2048]{2,1,0:T(8,128)} fusion(bf16[1024,512]{1,0:T(8,128)(2,1)} %get-tuple-element.6, bf16[1024,2048]{1,0:T(8,128)(2,1)} %get-tuple-element.7), kind=kOutput, calls=%fused_computation | convolution fusion | flops 2147483648 | bytes 9437184 | tf_op jit(solution)/shard_map/dot_general | solution.py:350
  195.3 0.0 copy-done
  195.3 1.0 copy.8
Async XLA Ops:
  188.3 7.0 %copy-start = (bf16[256,2048]{1,0:T(8,128)(2,1)S(1)}, bf16[256,2048]{1,0:T(8,128)(2,1)}, u32[]{:S(2)}) copy-start(bf16[256,2048]{1,0:T(8,128)(2,1)} %get-tuple-element.5) | copy-start | bytes 3145732

commit v3 on v2

--- a/solution.py
+++ b/solution.py
@@ -8,14 +8,13 @@
 from jax.sharding import PartitionSpec as P
 
 epsilon = 1e-05
-CHUNKS = 4
 TILE = 512
 PIECES = 4
 
 
 def relay_kernel(sections, replicas, blocks, ids_ref, epoch_ref, stream_ref, weight_whole, top_ref,
                  decoded_ref, normed_all, cot_all,
-                 weight, rows_in, normed, cot_in, cot_out, product, ahead, epoch,
+                 weight, rows_in, normed, cot_in, cot_out, product, ahead, turned, partial, epoch,
                  load_sem, w_send, w_recv, w_side_send, w_side_recv,
                  x_send, x_recv, g_send, g_recv, n_send, n_recv,
                  c_send, c_recv, c_side_send, c_side_recv, own_sem):
@@ -30,7 +29,8 @@
     weight_ref = weight_whole.at[0]
     shard = weight_ref.shape[0]
     span = width // PIECES
-    piece = shard // CHUNKS
+    chunks = w_send.shape[1]
+    piece = shard // chunks
     after, before = lax.rem(s + 1, sections), lax.rem(s + last, sections)
 
     def peer(offset):
@@ -96,19 +96,35 @@
         return remote(src, weight_rows(source(offset) + core, q),
                       w_side_send.at[offset, q], w_side_recv.at[offset, q], dp=sibling)
 
-    for q in range(CHUNKS):
+    for q in range(chunks):
         for offset in range(1, chips):
             weight_direct(offset, q).start()
         weight_side(0, q).start()
     epoch_load.start()
-    for q in range(CHUNKS):
+    def turn(owner, q):
+        first = pl.multiple_of(owner * shard + q * piece, piece)
+
+        def turn_columns(j, carry):
+            across = pl.ds(pl.multiple_of(j * TILE, TILE), TILE)
+            turned[across, pl.ds(first, piece)] = weight[pl.ds(first, piece), across].T
+            return carry
+
+        lax.fori_loop(0, width // TILE, turn_columns, 0)
+
+    shard_load.wait()
+    for q in range(chunks):
+        turn(me, q)
+    for q in range(chunks):
+        weight_side(0, q).wait_recv()
+        turn(sibling, q)
+    for q in range(chunks):
         for offset in range(1, chips):
             weight_direct(offset, q).wait_recv()
             weight_side(offset, q).start()
-    shard_load.wait()
-    for q in range(CHUNKS):
-        for offset in range(chips):
+            turn(source(offset) + core, q)
+        for offset in range(1, chips):
             weight_side(offset, q).wait_recv()
+            turn(source(offset) + 1 - core, q)
 
     @pl.when(s == 0)
     def _():
@@ -169,19 +185,25 @@
             total_squares += jnp.sum(part * part, axis=-1, keepdims=True)
         return lax.rsqrt(total_squares / width + epsilon)
 
+    def multiply(matrix, rows, result, m, p):
+        held = rows[block(m), columns(p)]
+        for start in range(0, width, TILE):
+            part = lax.dot_general(matrix[start:start + TILE, columns(p)], held,
+                                   (((1,), (1,)), ((), ())), preferred_element_type=jnp.float32)
+            if p > 0:
+                part += partial[start:start + TILE, :]
+            if p < PIECES - 1:
+                partial[start:start + TILE, :] = part
+            else:
+                result[block(m), start:start + TILE] = part.T
+
     def forward(m):
         for p in range(PIECES):
             @pl.when(s > 0)
             def _():
                 send_rows(m, p).wait_recv()
 
-            piece_rows = rows_in[block(m), columns(p)]
-            for start in range(0, width, TILE):
-                part = jnp.dot(piece_rows, weight[columns(p), start:start + TILE],
-                               preferred_element_type=jnp.float32)
-                if p > 0:
-                    part += product[block(m), start:start + TILE]
-                product[block(m), start:start + TILE] = part
+            multiply(turned, rows_in, product, m, p)
         scale = squared(m)
         squares = jnp.zeros((step_rows, 1), jnp.float32)
         for p in range(PIECES):
@@ -209,13 +231,7 @@
         for p in range(PIECES):
             if wait:
                 send_cot(m, p).wait_recv()
-            incoming = cot_in[block(m), columns(p)]
-            for start in range(0, width, TILE):
-                part = lax.dot_general(incoming, weight[start:start + TILE, columns(p)],
-                                       (((1,), (1,)), ((), ())), preferred_element_type=jnp.float32)
-                if p > 0:
-                    part += ahead[block(m), start:start + TILE]
-                ahead[block(m), start:start + TILE] = part
+            multiply(weight, cot_in, ahead, m, p)
 
     def backward(m):
         @pl.when((s < last) & (s > 0))
@@ -282,7 +298,7 @@
     for offset in range(1, replicas):
         send_normed(offset).wait_send()
         send_normed(offset).wait_recv()
-    for q in range(CHUNKS):
+    for q in range(chunks):
         for offset in range(1, chips):
             weight_direct(offset, q).wait_send()
         for offset in range(chips):
@@ -314,6 +330,7 @@
     total, width = stream_in.shape
     blocks = sample_ids.shape[1]
     shard = layer_weight.shape[1]
+    chunks = max(1, min(4, shard // 128))
     chips = replicas // 2
     dma = pltpu.SemaphoreType.DMA
     vmem = pl.BlockSpec(memory_space=pltpu.VMEM)
@@ -336,9 +353,11 @@
             pltpu.VMEM((total, width), jnp.bfloat16),
             pltpu.VMEM((total, width), jnp.float32),
             pltpu.VMEM((total, width), jnp.float32),
+            pltpu.VMEM((width, width), jnp.bfloat16),
+            pltpu.VMEM((width, total // blocks), jnp.float32),
             pltpu.VMEM(epoch_buffer.shape[1:], jnp.bfloat16),
             dma((5,)),
-            dma((far, CHUNKS)), dma((far, CHUNKS)), dma((chips, CHUNKS)), dma((chips, CHUNKS)),
+            dma((far, chunks)), dma((far, chunks)), dma((chips, chunks)), dma((chips, chunks)),
             dma((blocks, PIECES)), dma((blocks, PIECES)), dma((blocks, PIECES)), dma((blocks, PIECES)),
             dma((replicas - 1,)), dma((replicas - 1,)),
             dma((far, blocks)), dma((far, blocks)), dma((chips, blocks)), dma((chips, blocks)),

time: 196 us -> 208 us (1.061)
  Pallas kernels: 188 us -> 199 us
    pallas_call x1, Pallas kernels: 188 us -> 199 us  [local(): pl.pallas_call(functools.partial(relay_kernel, sections, replicas, blocks...]
where the time goes in v3:
time: 208 us
  Pallas kernels  199 us (96%)
  matrix products  6.98 us (3%)
    pallas_call x1, Pallas kernels, local(): pl.pallas_call(functools.partial(relay_kernel, sections, replicas, blocks...  199 us
    dot_general x1, matrix products, local(): lax.dot_general(normed_all, cot_all, (((0,), (0,)), ((), ())), preferred_...  6.98 us

profile of v3, /device:TPU:0, one launch (start us, length us, event | category | flops | bytes accessed | tf_op | source)
XLA Modules:
  0.0 208.0 jit_solution(2192237949873446244)
XLA Ops:
  0.6 199.4 %shard_map.68 = (bf16[256,2048]{1,0:T(8,128)(2,1)}, bf16[1024,512]{1,0:T(8,128)(2,1)}, bf16[1024,2048]{1,0:T(8,128)(2,1)}) custom-call(s32[1,8]{1,0:T(1,128)} %ids_ref.1, bf16[1,32,32,2048]{3,2,1,0:T(8,128)(2,1)} %epoch_ref.1, bf16[256,2048]{1,0:T(8,128)(2,1)} %stream_ref.1, bf16[1,512,2048]{2,1,0:T(8,128)(2,1)} %weight_whole.1, bf16[256,2048]{1,0:T(8,128)(2,1)} %top_ref.1), custom_call_target="tpu_custom_call" | custom-call | tf_op jit(solution)/shard_map/pallas_call | solution.py:339
  200.0 0.0 copy-start
  200.1 7.0 %convolution_bitcast_fusion = f32[1,512,2048]{2,1,0:T(8,128)} fusion(bf16[1024,512]{1,0:T(8,128)(2,1)} %get-tuple-element.6, bf16[1024,2048]{1,0:T(8,128)(2,1)} %get-tuple-element.7), kind=kOutput, calls=%fused_computation | convolution fusion | flops 2147483648 | bytes 9437184 | tf_op jit(solution)/shard_map/dot_general | solution.py:369
  207.0 0.0 copy-done
  207.0 1.0 copy.8
Async XLA Ops:
  200.0 7.0 %copy-start = (bf16[256,2048]{1,0:T(8,128)(2,1)S(1)}, bf16[256,2048]{1,0:T(8,128)(2,1)}, u32[]{:S(2)}) copy-start(bf16[256,2048]{1,0:T(8,128)(2,1)} %get-tuple-element.5) | copy-start | bytes 3145732

commit v4 on v2

--- a/solution.py
+++ b/solution.py
@@ -8,7 +8,6 @@
 from jax.sharding import PartitionSpec as P
 
 epsilon = 1e-05
-CHUNKS = 4
 TILE = 512
 PIECES = 4
 
@@ -30,7 +29,8 @@
     weight_ref = weight_whole.at[0]
     shard = weight_ref.shape[0]
     span = width // PIECES
-    piece = shard // CHUNKS
+    chunks = w_send.shape[1]
+    piece = shard // chunks
     after, before = lax.rem(s + 1, sections), lax.rem(s + last, sections)
 
     def peer(offset):
@@ -96,23 +96,39 @@
         return remote(src, weight_rows(source(offset) + core, q),
                       w_side_send.at[offset, q], w_side_recv.at[offset, q], dp=sibling)
 
-    for q in range(CHUNKS):
+    for q in range(chunks):
         for offset in range(1, chips):
             weight_direct(offset, q).start()
         weight_side(0, q).start()
     epoch_load.start()
-    for q in range(CHUNKS):
+    def absorb(first, depth):
+        @pl.when(s == 0)
+        def _():
+            lanes = pl.ds(pl.multiple_of(first, depth), depth)
+            for start in range(0, width, TILE):
+                product[:, start:start + TILE] += jnp.dot(
+                    rows_in[:, lanes], weight[lanes, start:start + TILE],
+                    preferred_element_type=jnp.float32)
+
+    @pl.when(s == 0)
+    def _():
+        stream_load.wait()
+        product[...] = jnp.zeros_like(product)
+
+    shard_load.wait()
+    absorb(me * shard, shard)
+    for q in range(chunks):
+        weight_side(0, q).wait_recv()
+    absorb(sibling * shard, shard)
+    for q in range(chunks):
         for offset in range(1, chips):
             weight_direct(offset, q).wait_recv()
             weight_side(offset, q).start()
-    shard_load.wait()
-    for q in range(CHUNKS):
-        for offset in range(chips):
+        for offset in range(1, chips):
+            absorb((source(offset) + core) * shard + q * piece, piece)
+        for offset in range(1, chips):
             weight_side(offset, q).wait_recv()
-
-    @pl.when(s == 0)
-    def _():
-        stream_load.wait()
+            absorb((source(offset) + 1 - core) * shard + q * piece, piece)
 
     @pl.when(s == last)
     def _():
@@ -170,18 +186,18 @@
         return lax.rsqrt(total_squares / width + epsilon)
 
     def forward(m):
-        for p in range(PIECES):
-            @pl.when(s > 0)
-            def _():
+        @pl.when(s > 0)
+        def _():
+            for p in range(PIECES):
                 send_rows(m, p).wait_recv()
-
-            piece_rows = rows_in[block(m), columns(p)]
-            for start in range(0, width, TILE):
-                part = jnp.dot(piece_rows, weight[columns(p), start:start + TILE],
-                               preferred_element_type=jnp.float32)
-                if p > 0:
-                    part += product[block(m), start:start + TILE]
-                product[block(m), start:start + TILE] = part
+                piece_rows = rows_in[block(m), columns(p)]
+                for start in range(0, width, TILE):
+                    part = jnp.dot(piece_rows, weight[columns(p), start:start + TILE],
+                                   preferred_element_type=jnp.float32)
+                    if p > 0:
+                        part += product[block(m), start:start + TILE]
+                    product[block(m), start:start + TILE] = part
+
         scale = squared(m)
         squares = jnp.zeros((step_rows, 1), jnp.float32)
         for p in range(PIECES):
@@ -282,7 +298,7 @@
     for offset in range(1, replicas):
         send_normed(offset).wait_send()
         send_normed(offset).wait_recv()
-    for q in range(CHUNKS):
+    for q in range(chunks):
         for offset in range(1, chips):
             weight_direct(offset, q).wait_send()
         for offset in range(chips):
@@ -310,10 +326,19 @@
     lax.fori_loop(0, blocks, finish, 0)
 
 
+def gradient_kernel(normed_ref, cot_ref, gradient_ref, flipped):
+    @pl.when(pl.program_id(0) == 0)
+    def _():
+        flipped[...] = normed_ref[...].T
+
+    gradient_ref[...] = jnp.dot(flipped[...], cot_ref[...], preferred_element_type=jnp.float32)
+
+
 def local(sections, replicas, stream_in, sample_ids, epoch_buffer, layer_weight, top_cotangent):
     total, width = stream_in.shape
     blocks = sample_ids.shape[1]
     shard = layer_weight.shape[1]
+    chunks = max(1, min(4, shard // 128))
     chips = replicas // 2
     dma = pltpu.SemaphoreType.DMA
     vmem = pl.BlockSpec(memory_space=pltpu.VMEM)
@@ -338,7 +363,7 @@
             pltpu.VMEM((total, width), jnp.float32),
             pltpu.VMEM(epoch_buffer.shape[1:], jnp.bfloat16),
             dma((5,)),
-            dma((far, CHUNKS)), dma((far, CHUNKS)), dma((chips, CHUNKS)), dma((chips, CHUNKS)),
+            dma((far, chunks)), dma((far, chunks)), dma((chips, chunks)), dma((chips, chunks)),
             dma((blocks, PIECES)), dma((blocks, PIECES)), dma((blocks, PIECES)), dma((blocks, PIECES)),
             dma((replicas - 1,)), dma((replicas - 1,)),
             dma((far, blocks)), dma((far, blocks)), dma((chips, blocks)), dma((chips, blocks)),
@@ -347,8 +372,18 @@
         compiler_params=pltpu.CompilerParams(
             collective_id=0, has_side_effects=True, vmem_limit_bytes=60 * 1024 * 1024),
     )(sample_ids, epoch_buffer, stream_in, layer_weight, top_cotangent)
-    gradient = lax.dot_general(
-        normed_all, cot_all, (((0,), (0,)), ((), ())), preferred_element_type=jnp.float32)
+    gradient = pl.pallas_call(
+        gradient_kernel,
+        grid=(width // TILE,),
+        out_shape=jax.ShapeDtypeStruct((shard, width), jnp.float32),
+        in_specs=[
+            pl.BlockSpec((replicas * total, shard), lambda j: (0, 0)),
+            pl.BlockSpec((replicas * total, TILE), lambda j: (0, j)),
+        ],
+        out_specs=pl.BlockSpec((shard, TILE), lambda j: (0, j)),
+        scratch_shapes=[pltpu.VMEM((shard, replicas * total), jnp.bfloat16)],
+        compiler_params=pltpu.CompilerParams(vmem_limit_bytes=60 * 1024 * 1024),
+    )(normed_all, cot_all)
     return (decoded[None], gradient[None])
 
 

time: 196 us -> 196 us (level)
  matrix products: 6.98 us -> 0 us
  Pallas kernels: 188 us -> 194 us
    dot_general x1 -> x0, matrix products: 6.98 us -> none  [local(): lax.dot_general(normed_all, cot_all, (((0,), (0,)), ((), ())), preferred_...]
    pallas_call x0 -> x1, Pallas kernels: none -> 6.78 us  [local(): pl.pallas_call(gradient_kernel, grid=(width // TILE,), out_shape=jax.Shap...]
where the time goes in v4:
time: 196 us
  Pallas kernels  194 us (99%)
    pallas_call x1, Pallas kernels, local(): pl.pallas_call(functools.partial(relay_kernel, sections, replicas, blocks...  187 us
    pallas_call x1, Pallas kernels, local(): pl.pallas_call(gradient_kernel, grid=(width // TILE,), out_shape=jax.Shap...  6.78 us

profile of v4, /device:TPU:0, one launch (start us, length us, event | category | flops | bytes accessed | tf_op | source)
XLA Modules:
  0.0 195.8 jit_solution(14969364454423658782)
XLA Ops:
  0.6 187.4 %shard_map.68 = (bf16[256,2048]{1,0:T(8,128)(2,1)}, bf16[1024,512]{1,0:T(8,128)(2,1)}, bf16[1024,2048]{1,0:T(8,128)(2,1)}) custom-call(s32[1,8]{1,0:T(1,128)} %ids_ref.1, bf16[1,32,32,2048]{3,2,1,0:T(8,128)(2,1)} %epoch_ref.1, bf16[256,2048]{1,0:T(8,128)(2,1)} %stream_ref.1, bf16[1,512,2048]{2,1,0:T(8,128)(2,1)} %weight_whole.1, bf16[256,2048]{1,0:T(8,128)(2,1)} %top_ref.1), custom_call_target="tpu_custom_call" | custom-call | tf_op jit(solution)/shard_map/pallas_call | solution.py:347
  188.0 0.0 copy-start
  188.0 6.8 %shard_map.69 = f32[512,2048]{1,0:T(8,128)} custom-call(bf16[1024,512]{1,0:T(8,128)(2,1)} %get-tuple-element.6.normed_ref, bf16[1024,2048]{1,0:T(8,128)(2,1)} %get-tuple-element.7.cot_ref), custom_call_target="tpu_custom_call" | custom-call | tf_op jit(solution)/shard_map/pallas_call | solution.py:375
  194.8 0.0 copy-done
  194.8 1.0 copy.8
Async XLA Ops:
  188.0 6.8 %copy-start = (bf16[256,2048]{1,0:T(8,128)(2,1)S(1)}, bf16[256,2048]{1,0:T(8,128)(2,1)}, u32[]{:S(2)}) copy-start(bf16[256,2048]{1,0:T(8,128)(2,1)} %get-tuple-element.5) | copy-start | bytes 3145732

commit v5 on v4

--- a/solution.py
+++ b/solution.py
@@ -185,46 +185,50 @@
             total_squares += jnp.sum(part * part, axis=-1, keepdims=True)
         return lax.rsqrt(total_squares / width + epsilon)
 
-    def forward(m):
+    def forward(m, count):
+        group = pl.ds(pl.multiple_of(m * step_rows, step_rows), count * step_rows)
+
         @pl.when(s > 0)
         def _():
             for p in range(PIECES):
-                send_rows(m, p).wait_recv()
-                piece_rows = rows_in[block(m), columns(p)]
+                for i in range(count):
+                    send_rows(m + i, p).wait_recv()
+                piece_rows = rows_in[group, columns(p)]
                 for start in range(0, width, TILE):
                     part = jnp.dot(piece_rows, weight[columns(p), start:start + TILE],
                                    preferred_element_type=jnp.float32)
                     if p > 0:
-                        part += product[block(m), start:start + TILE]
-                    product[block(m), start:start + TILE] = part
-
-        scale = squared(m)
-        squares = jnp.zeros((step_rows, 1), jnp.float32)
+                        part += product[group, start:start + TILE]
+                    product[group, start:start + TILE] = part
+
+        for i in range(count):
+            scale = squared(m + i)
+            squares = jnp.zeros((step_rows, 1), jnp.float32)
+            for p in range(PIECES):
+                values = rows_in[block(m + i), columns(p)].astype(jnp.float32)
+                part = values + scale * product[block(m + i), columns(p)]
+                product[block(m + i), columns(p)] = part
+                squares += jnp.sum(part * part, axis=-1, keepdims=True)
+            bound = 2.0 * jnp.sqrt(squares / width + epsilon)
+            entry = ids_ref[0, m + i]
+            for p in range(PIECES):
+                base = epoch[entry, :, columns(p)].astype(jnp.float32)
+                delta = jnp.clip(product[block(m + i), columns(p)] - base, -bound, bound).astype(
+                    jnp.bfloat16)
+                decoded_ref[block(m + i), columns(p)] = (
+                    base + delta.astype(jnp.float32)).astype(jnp.bfloat16)
+
+                @pl.when(s < last)
+                def _():
+                    send_rows(m + i, p).start()
+
+            for p in range(PIECES):
+                values = rows_in[block(m + i), columns(p)].astype(jnp.float32)
+                normed[block(m + i), columns(p)] = (values * scale).astype(jnp.bfloat16)
+
+    def back_product(m):
         for p in range(PIECES):
-            values = rows_in[block(m), columns(p)].astype(jnp.float32)
-            part = values + scale * product[block(m), columns(p)]
-            product[block(m), columns(p)] = part
-            squares += jnp.sum(part * part, axis=-1, keepdims=True)
-        bound = 2.0 * jnp.sqrt(squares / width + epsilon)
-        entry = ids_ref[0, m]
-        for p in range(PIECES):
-            base = epoch[entry, :, columns(p)].astype(jnp.float32)
-            delta = jnp.clip(product[block(m), columns(p)] - base, -bound, bound).astype(jnp.bfloat16)
-            decoded_ref[block(m), columns(p)] = (
-                base + delta.astype(jnp.float32)).astype(jnp.bfloat16)
-
-            @pl.when(s < last)
-            def _():
-                send_rows(m, p).start()
-
-        for p in range(PIECES):
-            values = rows_in[block(m), columns(p)].astype(jnp.float32)
-            normed[block(m), columns(p)] = (values * scale).astype(jnp.bfloat16)
-
-    def back_product(m, wait):
-        for p in range(PIECES):
-            if wait:
-                send_cot(m, p).wait_recv()
+            send_cot(m, p).wait_recv()
             incoming = cot_in[block(m), columns(p)]
             for start in range(0, width, TILE):
                 part = lax.dot_general(incoming, weight[start:start + TILE, columns(p)],
@@ -236,7 +240,7 @@
     def backward(m):
         @pl.when((s < last) & (s > 0))
         def _():
-            back_product(m, True)
+            back_product(m)
 
         @pl.when(s == 0)
         def _():
@@ -270,14 +274,23 @@
 
     @pl.when(s == last)
     def _():
-        lax.fori_loop(0, blocks, lambda m, carry: (back_product(m, False), carry)[1], 0)
-
-    lag = jnp.minimum(blocks, (last - s) * 3)
+        for start in range(0, width, TILE):
+            ahead[:, start:start + TILE] = lax.dot_general(
+                cot_in[...], weight[start:start + TILE, :], (((1,), (1,)), ((), ())),
+                preferred_element_type=jnp.float32)
+
+    wide = 2 - blocks % 2
+    paired = s >= last - 1
+    lag = jnp.minimum(blocks, jnp.maximum((last - s) * 3, wide - 1))
 
     def step(k, carry):
-        @pl.when(k < blocks)
-        def _():
-            forward(k)
+        @pl.when((k < blocks) & jnp.logical_not(paired))
+        def _():
+            forward(k, 1)
+
+        @pl.when((k < blocks) & paired & (k % wide == wide - 1))
+        def _():
+            forward(k - (wide - 1), wide)
 
         @pl.when(k == blocks - 1)
         def _():

time: 196 us -> 195 us (level)
  no operation moved by 1% of the time
where the time goes in v5:
time: 195 us
  Pallas kernels  193 us (99%)
    pallas_call x1, Pallas kernels, local(): pl.pallas_call(functools.partial(relay_kernel, sections, replicas, blocks...  186 us
    pallas_call x1, Pallas kernels, local(): pl.pallas_call(gradient_kernel, grid=(width // TILE,), out_shape=jax.Shap...  6.78 us

profile of v5, /device:TPU:0, one launch (start us, length us, event | category | flops | bytes accessed | tf_op | source)
XLA Modules:
  0.0 194.5 jit_solution(14870142852822695960)
XLA Ops:
  0.6 186.1 %shard_map.68 = (bf16[256,2048]{1,0:T(8,128)(2,1)}, bf16[1024,512]{1,0:T(8,128)(2,1)}, bf16[1024,2048]{1,0:T(8,128)(2,1)}) custom-call(s32[1,8]{1,0:T(1,128)} %ids_ref.1, bf16[1,32,32,2048]{3,2,1,0:T(8,128)(2,1)} %epoch_ref.1, bf16[256,2048]{1,0:T(8,128)(2,1)} %stream_ref.1, bf16[1,512,2048]{2,1,0:T(8,128)(2,1)} %weight_whole.1, bf16[256,2048]{1,0:T(8,128)(2,1)} %top_ref.1), custom_call_target="tpu_custom_call" | custom-call | tf_op jit(solution)/shard_map/pallas_call | solution.py:360
  186.7 0.0 copy-start
  186.8 6.8 %shard_map.69 = f32[512,2048]{1,0:T(8,128)} custom-call(bf16[1024,512]{1,0:T(8,128)(2,1)} %get-tuple-element.6.normed_ref, bf16[1024,2048]{1,0:T(8,128)(2,1)} %get-tuple-element.7.cot_ref), custom_call_target="tpu_custom_call" | custom-call | tf_op jit(solution)/shard_map/pallas_call | solution.py:388
  193.5 0.0 copy-done
  193.5 1.0 copy.8
Async XLA Ops:
  186.7 6.8 %copy-start = (bf16[256,2048]{1,0:T(8,128)(2,1)S(1)}, bf16[256,2048]{1,0:T(8,128)(2,1)}, u32[]{:S(2)}) copy-start(bf16[256,2048]{1,0:T(8,128)(2,1)} %get-tuple-element.5) | copy-start | bytes 3145732

commit v6 on v5

--- a/solution.py
+++ b/solution.py
@@ -9,7 +9,7 @@
 
 epsilon = 1e-05
 TILE = 512
-PIECES = 4
+PIECES = 2
 
 
 def relay_kernel(sections, replicas, blocks, ids_ref, epoch_ref, stream_ref, weight_whole, top_ref,

time: 195 us -> 199 us (1.021)
  Pallas kernels: 193 us -> 197 us
    pallas_call x1, Pallas kernels: 186 us -> 190 us  [local(): pl.pallas_call(functools.partial(relay_kernel, sections, replicas, blocks...]
where the time goes in v6:
time: 199 us
  Pallas kernels  197 us (99%)
    pallas_call x1, Pallas kernels, local(): pl.pallas_call(functools.partial(relay_kernel, sections, replicas, blocks...  190 us
    pallas_call x1, Pallas kernels, local(): pl.pallas_call(gradient_kernel, grid=(width // TILE,), out_shape=jax.Shap...  6.79 us

profile of v6, /device:TPU:0, one launch (start us, length us, event | category | flops | bytes accessed | tf_op | source)
XLA Modules:
  0.0 198.7 jit_solution(131678293693226709)
XLA Ops:
  0.6 190.3 %shard_map.68 = (bf16[256,2048]{1,0:T(8,128)(2,1)}, bf16[1024,512]{1,0:T(8,128)(2,1)}, bf16[1024,2048]{1,0:T(8,128)(2,1)}) custom-call(s32[1,8]{1,0:T(1,128)} %ids_ref.1, bf16[1,32,32,2048]{3,2,1,0:T(8,128)(2,1)} %epoch_ref.1, bf16[256,2048]{1,0:T(8,128)(2,1)} %stream_ref.1, bf16[1,512,2048]{2,1,0:T(8,128)(2,1)} %weight_whole.1, bf16[256,2048]{1,0:T(8,128)(2,1)} %top_ref.1), custom_call_target="tpu_custom_call" | custom-call | tf_op jit(solution)/shard_map/pallas_call | solution.py:360
  190.9 0.0 copy-start
  190.9 6.8 %shard_map.69 = f32[512,2048]{1,0:T(8,128)} custom-call(bf16[1024,512]{1,0:T(8,128)(2,1)} %get-tuple-element.6.normed_ref, bf16[1024,2048]{1,0:T(8,128)(2,1)} %get-tuple-element.7.cot_ref), custom_call_target="tpu_custom_call" | custom-call | tf_op jit(solution)/shard_map/pallas_call | solution.py:388
  197.7 0.0 copy-done
  197.7 1.0 copy.8
Async XLA Ops:
  190.9 6.8 %copy-start = (bf16[256,2048]{1,0:T(8,128)(2,1)S(1)}, bf16[256,2048]{1,0:T(8,128)(2,1)}, u32[]{:S(2)}) copy-start(bf16[256,2048]{1,0:T(8,128)(2,1)} %get-tuple-element.5) | copy-start | bytes 3145732
